TPU v7x, 128 devices: a whole 4x4x4 slice. The times are simulated.
128 devices in a mesh: ctx: 64 (over y, x, z), head: 2 (over core).
Axes of the slice: x: 4, y: 4, z: 4, core: 2. Of those that a mesh axis runs over, the one named last changes fastest.
Arguments:
- queries: bfloat16 [32768, 4096], P('ctx', 'head'), may hold values from -24 to 24
- keys: bfloat16 [32768, 1024], P('ctx', 'head'), may hold values from -24 to 24
- values: bfloat16 [32768, 1024], P('ctx', 'head'), may hold values from -40 to 40
- token_log_decay: float32 [8, 32768], P('head', 'ctx'), may hold values from -1 to 0
- seq_ids: int32 [32768], P('ctx'), may hold values from 0 to 7, never falling along the last dimension, each value on 1 to 24576 neighbouring positions
- norm_gain: float32 [4096], P('head'), may hold values from 0.1 to 0.4
Outputs:
- combined: bfloat16 [32768, 4096], P('ctx', 'head')
Inputs may be any that keep to these rules, and one draw needn't show every extreme that they name: `seq_ids`: each sequence is one contiguous run of tokens and the numbers never fall; no run is longer than 24576 tokens and one has exactly 24576.
All inputs are finite; a program needn't handle non-finite values.
Results may differ from a plain program's by a relative error of at most 0.0075.
Values may be sent and summed in bfloat16 or wider, within the bound.
A program may use at most 192 MiB of HBM per device.

v0:
```python
import math

import jax
import jax.numpy as jnp
from jax import lax
from jax.sharding import PartitionSpec as P

QUERY_HEADS = 32
KEY_VALUE_HEADS = 8
HEAD_SIZE = 128
WINDOW_LENGTH = 2048


def shifted(value, axis, steps):
    count = lax.axis_size(axis)
    first, last = (max(0, -steps), min(count, count - steps))
    return lax.ppermute(value, axis, [(source, source + steps) for source in range(first, last)])


def body(queries, keys, values, token_log_decay, seq_ids, norm_gain):
    tok_rows = queries.shape[0]
    query_groups = QUERY_HEADS // KEY_VALUE_HEADS
    local_kv = keys.shape[1] // HEAD_SIZE
    reach_shards = WINDOW_LENGTH // tok_rows
    id_marks = seq_ids.astype(jnp.bfloat16)
    own_piece = (keys, values, id_marks)
    received = []
    for shift_by in range(1, reach_shards + 1):
        received.append(shifted((keys, values, id_marks), "ctx", shift_by))
    prev_id = received[0][2][tok_rows - 1].astype(jnp.int32)
    key_order = [received[shard_back] for shard_back in range(reach_shards - 1, -1, -1)] + [
        own_piece
    ]
    all_keys = jnp.concatenate([entry[0] for entry in key_order], 0)
    all_values = jnp.concatenate([entry[1] for entry in key_order], 0)
    key_ids = jnp.concatenate([entry[2] for entry in key_order], 0).astype(jnp.int32)
    ctx_index = lax.axis_index("ctx")
    q_pos = ctx_index * tok_rows + jnp.arange(tok_rows, dtype=jnp.int32)
    k_pos = (ctx_index - reach_shards) * tok_rows + jnp.arange(
        (reach_shards + 1) * tok_rows, dtype=jnp.int32
    )
    distance = q_pos[:, None] - k_pos[None, :]
    allowed = (
        (k_pos[None, :] >= 0)
        & (distance >= 0)
        & (distance < WINDOW_LENGTH)
        & (seq_ids[:, None] == key_ids[None, :])
    )
    allowed = allowed[:, None, :]
    score_scale = 1.0 / math.sqrt(HEAD_SIZE)
    head_outputs = []
    for kv_head in range(local_kv):
        q_head = queries[
            :, kv_head * query_groups * HEAD_SIZE : (kv_head + 1) * query_groups * HEAD_SIZE
        ].reshape(tok_rows, query_groups, HEAD_SIZE)
        k_head = all_keys[:, kv_head * HEAD_SIZE : (kv_head + 1) * HEAD_SIZE]
        v_head = all_values[:, kv_head * HEAD_SIZE : (kv_head + 1) * HEAD_SIZE]
        scores = (
            jnp.einsum("tgd,kd->tgk", q_head, k_head, preferred_element_type=jnp.float32)
            * score_scale
        )
        scores = jnp.where(allowed, scores, -1e30)
        row_max = jnp.max(scores, axis=2, keepdims=True)
        exp_scores = jnp.where(allowed, jnp.exp(scores - row_max), 0.0)
        weights = (exp_scores / jnp.sum(exp_scores, axis=2, keepdims=True)).astype(jnp.bfloat16)
        head_out = jnp.einsum("tgk,kd->tgd", weights, v_head, preferred_element_type=jnp.float32)
        head_outputs.append(head_out.reshape(tok_rows, query_groups * HEAD_SIZE))
    window_out = jnp.concatenate(head_outputs, 1)
    q_grouped = queries.reshape(tok_rows, local_kv, query_groups, HEAD_SIZE)
    k_heads = keys.reshape(tok_rows, local_kv, HEAD_SIZE)
    v_heads = values.reshape(tok_rows, local_kv, HEAD_SIZE)
    k_float = k_heads.astype(jnp.float32)
    v_float = v_heads.astype(jnp.float32)
    cumulative = jnp.cumsum(token_log_decay, axis=1)
    positions = jnp.arange(tok_rows, dtype=jnp.int32)
    lower_mask = positions[:, None] >= positions[None, :]
    linked = lower_mask & (seq_ids[:, None] == seq_ids[None, :])
    exponent = jnp.where(linked[None], cumulative[:, :, None] - cumulative[:, None, :], 0.0)
    decays = jnp.where(linked[None], jnp.exp(exponent), 0.0)
    qk_dots = jnp.einsum("thgd,shd->hgts", q_grouped, k_heads, preferred_element_type=jnp.float32)
    inner_term = jnp.einsum(
        "hgts,shd->thgd", qk_dots * decays[:, None], v_float, precision=lax.Precision.HIGHEST
    )
    last_id = seq_ids[tok_rows - 1]
    tail_weight = jnp.where(
        seq_ids[None, :] == last_id, jnp.exp(cumulative[:, -1:] - cumulative), 0.0
    )
    local_state = jnp.einsum(
        "shd,she->hde",
        k_float * tail_weight.T[:, :, None],
        v_float,
        precision=lax.Precision.HIGHEST,
    )
    carry_factor = jnp.exp(cumulative[:, -1]) * (last_id == prev_id).astype(jnp.float32)
    ctx_count = lax.axis_size("ctx")
    factors = lax.all_gather(carry_factor[None, :], "ctx", axis=0, tiled=True)
    dev_index = jnp.arange(ctx_count, dtype=jnp.int32)[:, None]
    passed = jnp.where(dev_index < ctx_index, factors, 1.0)
    suffix = jnp.flip(jnp.cumprod(jnp.flip(passed, 0), axis=0), 0)
    coefficients = jnp.concatenate([suffix[1:], jnp.ones_like(suffix[:1])], 0)
    coefficients = jnp.where(dev_index < ctx_index, coefficients, 0.0)
    incoming = jnp.zeros_like(local_state) + jnp.sum(
        coefficients[:, :, None, None]
        * lax.all_gather(local_state[None].astype(jnp.bfloat16), "ctx", axis=0, tiled=True).astype(
            jnp.float32
        ),
        axis=0,
    )
    entry_factor = jnp.exp(cumulative) * (seq_ids == prev_id)[None, :].astype(jnp.float32)
    cross_term = (
        jnp.einsum(
            "thgd,hde->thge",
            q_grouped.astype(jnp.float32),
            incoming,
            precision=lax.Precision.HIGHEST,
        )
        * entry_factor.T[:, :, None, None]
    )
    linear_out = (inner_term + cross_term).reshape(tok_rows, local_kv * query_groups * HEAD_SIZE)
    squares = jnp.sum(linear_out * linear_out, axis=1)
    sum_total = lax.psum(squares, "head")
    normed = linear_out * lax.rsqrt(sum_total / (QUERY_HEADS * HEAD_SIZE) + 1e-06)[:, None]
    return (window_out + norm_gain[None, :] * normed).astype(jnp.bfloat16)


def solution(mesh):
    return jax.shard_map(
        body,
        mesh=mesh,
        in_specs=(
            P("ctx", "head"),
            P("ctx", "head"),
            P("ctx", "head"),
            P("head", "ctx"),
            P("ctx"),
            P("head"),
        ),
        out_specs=P("ctx", "head"),
        check_vma=False,
    )
```

profile of v0, /device:TPU:1, one launch (start us, length us, event | category | flops | bytes accessed | tf_op | source)
XLA Modules:
  0.0 425.7 jit_solution(12679538010600954295)
XLA Ops:
  7.2 3.9 collective-permute-start
  11.2 5.7 %collective-permute-start.1 = (bf16[512]{0:T(512)(128)(2,1)S(1)}, bf16[512]{0:T(512)(128)(2,1)S(1)}, u32[]{:S(2)}, u32[]{:S(2)}) collective-permute-start(bf16[512]{0:T(512)(128)(2,1)S(1)} %convert_element_type.52), channel_id=1, source_target_pairs={{0,6},{2,8},{4,10},{6,12},{8,14},{10,16},{12,18},{14,20},{16,22},{... | collective-permute-start | bytes 3080 | tf_op jit(solution)/shard_map/ppermute | solution.py:17
  16.8 2.5 collective-permute-start.2
  19.3 2.9 collective-permute-start.3
  22.3 3.6 collective-permute-start.4
  25.9 1.3 slice.73
  27.3 1.2 reshape.271
  28.5 2.9 fusion.65
  31.4 3.2 reshape.272
  34.9 1.2 reduce-window.6
  36.6 1.1 copy.79
  37.7 2.7 exponential_select_fusion.4
  40.5 8.2 %fusion.42 = f32[4,512,512,4]{2,1,3,0:T(8,128)} fusion(bf16[512,4,4,128]{3,2,1,0:T(4,128)(2,1)S(1)} %reshape.272, bf16[512,4,128,1]{2,1,0,3:T(4,128)(2,1)S(1)} %bitcast.174), kind=kOutput, calls=%fused_computation.58 | convolution fusion | flops 1073741824 | bytes 19398656 | tf_op jit(solution)/shard_map/thgd,shd->hgts/dot_general | solution.py:80
  49.9 2.1 copy.102
  52.0 2.1 copy.103
  57.4 5.3 %collective-permute-start.5 = (bf16[512,512]{1,0:T(8,128)(2,1)S(1)}, bf16[512,512]{1,0:T(8,128)(2,1)}, u32[]{:S(2)}, u32[]{:S(2)}) collective-permute-start(bf16[512,512]{1,0:T(8,128)(2,1)S(1)} %copy-done.5), channel_id=1, source_target_pairs={{0,6},{2,8},{4,10},{6,12},{8,14},{10,16},{12,18},{14,20},{16,22},{... | collective-permute-start | bytes 1572872 | tf_op jit(solution)/shard_map/ppermute | solution.py:17
  65.3 4.1 collective-permute-start.6
  69.6 2.1 collective-permute-start.7
  71.8 2.3 collective-permute-start.8
  75.1 1.3 convolution_convert_fusion
  76.5 2.7 fusion.29
  79.3 154.7 %all-reduce.1 = f32[256]{0:T(256)S(1)} all-reduce(f32[256]{0:T(256)S(1)} %bitcast_dynamic-update-slice_fusion), channel_id=2, replica_groups=mesh['ctx'=64,'head'=2] {'ctx'}, use_global_device_ids=true, to_apply=%add.1 | all-reduce | flops 256 | bytes 2048
  235.0 2.1 collective-permute-start.9
  238.2 2.1 collective-permute-start.10
  241.3 4.6 %collective-permute-start.11 = (bf16[512,512]{0,1:T(8,128)(2,1)S(1)}, bf16[512,512]{0,1:T(8,128)(2,1)}, u32[]{:S(2)}, u32[]{:S(2)}) collective-permute-start(bf16[512,512]{0,1:T(8,128)(2,1)S(1)} %copy.55), channel_id=1, source_target_pairs={{0,2},{2,4},{4,6},{6,8},{8,10},{10,12},{12,14},{14,16},{16,18},{18... | collective-permute-start | bytes 1572872 | tf_op jit(solution)/shard_map/ppermute | solution.py:17
  245.9 1.1 constant_dynamic-update-slice_fusion.7
  247.0 1.1 constant_dynamic-update-slice_fusion.6
  248.2 1.4 copy-done.14
  249.6 14.3 %fusion.69 = (f32[512,4]{0,1:T(4,128)S(1)}, f32[512,4,2560]{0,2,1:T(8,128)}) fusion(pred[512,2560]{0,1:T(8,128)(4,1)S(1)} %fusion.29, bf16[512,4,128]{0,2,1:T(8,128)(2,1)S(1)} %bitcast.183, bf16[2560,512]{1,0:T(8,128)(2,1)} %copy-done.14), kind=kOutput, calls=%fused_computation.121 | convolution fusion | flops 1368394240 | bytes 24780800 | tf_op jit(solution)/shard_map/sub | solution.py:64
  265.0 1.1 constant_dynamic-update-slice_fusion.3
  266.1 1.1 constant_dynamic-update-slice_fusion.2
  267.1 1.1 constant_dynamic-update-slice_fusion.1
  268.3 8.9 %fusion.22 = f32[512,4,128]{0,2,1:T(8,128)S(1)} fusion(f32[512,4,2560]{0,2,1:T(8,128)} %get-tuple-element.20, f32[512,4]{0,1:T(4,128)S(1)} %get-tuple-element.19, bf16[2560,512]{0,1:T(8,128)(2,1)S(1)} %constant_dynamic-update-slice_fusion), kind=kOutput, calls=%fused_computation.36 | convolution fusion | flops 1352663040 | bytes 22683648 | tf_op jit(solution)/shard_map/tgk,kd->tgd/dot_general | solution.py:66
  277.6 14.5 %fusion.68 = (f32[512,4]{0,1:T(4,128)S(1)}, f32[512,4,2560]{0,2,1:T(8,128)}) fusion(pred[512,2560]{0,1:T(8,128)(4,1)S(1)} %copy-done.9, bf16[512,4,128]{0,2,1:T(8,128)(2,1)} %bitcast.182, bf16[2560,512]{1,0:T(8,128)(2,1)} %copy-done.14), kind=kOutput, calls=%fused_computation.120 | convolution fusion | flops 1368394240 | bytes 24780800 | tf_op jit(solution)/shard_map/sub | solution.py:64
  292.1 9.7 %fusion.23 = f32[512,4,128]{0,2,1:T(8,128)} fusion(f32[512,4,2560]{0,2,1:T(8,128)} %get-tuple-element.18, f32[512,4]{0,1:T(4,128)S(1)} %get-tuple-element.17, bf16[2560,512]{0,1:T(8,128)(2,1)} %copy-done.15), kind=kOutput, calls=%fused_computation.37 | convolution fusion | flops 1352663040 | bytes 22683648 | tf_op jit(solution)/shard_map/tgk,kd->tgd/dot_general | solution.py:66
  301.8 1.6 copy.71
  303.4 14.3 %fusion.67 = (f32[512,4]{0,1:T(4,128)S(1)}, f32[512,4,2560]{0,2,1:T(8,128)}) fusion(pred[512,2560]{0,1:T(8,128)(4,1)S(1)} %copy-done.9, bf16[512,4,128]{0,2,1:T(8,128)(2,1)} %bitcast.181, bf16[2560,512]{1,0:T(8,128)(2,1)} %copy-done.14), kind=kOutput, calls=%fused_computation.119 | convolution fusion | flops 1368394240 | bytes 24780800 | tf_op jit(solution)/shard_map/sub | solution.py:64
  317.7 9.7 %fusion.24 = f32[512,4,128]{0,2,1:T(8,128)} fusion(f32[512,4,2560]{0,2,1:T(8,128)} %get-tuple-element.16, f32[512,4]{0,1:T(4,128)S(1)} %get-tuple-element.15, bf16[2560,512]{0,1:T(8,128)(2,1)} %copy-done.15), kind=kOutput, calls=%fused_computation.38 | convolution fusion | flops 1352663040 | bytes 22683648 | tf_op jit(solution)/shard_map/tgk,kd->tgd/dot_general | solution.py:66
  327.4 1.6 copy.72
  329.0 15.2 %fusion.66 = (f32[512,4]{0,1:T(4,128)S(1)}, f32[512,4,2560]{0,2,1:T(8,128)}) fusion(pred[512,2560]{0,1:T(8,128)(4,1)} %copy-done.8, bf16[512,4,128]{0,2,1:T(8,128)(2,1)} %bitcast.180, bf16[2560,512]{1,0:T(8,128)(2,1)} %copy-done.14), kind=kOutput, calls=%fused_computation.118 | convolution fusion | flops 1368394240 | bytes 24780800 | tf_op jit(solution)/shard_map/sub | solution.py:64
  344.2 9.7 %fusion.25 = f32[512,4,128]{0,2,1:T(8,128)} fusion(f32[512,4,2560]{0,2,1:T(8,128)} %get-tuple-element.14, f32[512,4]{0,1:T(4,128)S(1)} %get-tuple-element.13, bf16[2560,512]{0,1:T(8,128)(2,1)} %copy-done.15), kind=kOutput, calls=%fused_computation.39 | convolution fusion | flops 1352663040 | bytes 22683648 | tf_op jit(solution)/shard_map/tgk,kd->tgd/dot_general | solution.py:66
  353.9 2.6 copy.73
  356.5 5.2 %fusion.4 = f32[4,128,128]{2,1,0:T(8,128)S(1)} fusion(bf16[64,4,128,128]{3,2,1,0:T(8,128)(2,1)} %bitcast.173, f32[64,4]{1,0:T(8,128)S(1)} %copy-done.13), kind=kLoop, calls=%fused_computation.17 | loop fusion | flops 12517376 | bytes 8651776 | tf_op jit(solution)/shard_map/reduce_sum | solution.py:102
  361.8 2.4 fusion.40
  364.2 12.4 %multiply_reduce_fusion = (f32[512]{0:T(512)S(1)}, f32[512,4,4,128]{0,3,2,1:T(8,128)}) fusion(f32[512,4]{0,1:T(4,128)S(1)} %copy-done.12, f32[4,128,512,4]{2,1,3,0:T(8,128)S(1)} %fusion.40, bf16[512,4,128,1]{2,1,0,3:T(4,128)(2,1)S(1)} %bitcast.175, f32[4,512,512,4]{2,1,3,0:T(8,128)} %fusion.42, f32[4,512,512]{1,2,0:T(8,128)S(1)} %copy-done.2), kind=kOutput, calls=%fused_computation.50 | convolution fusion | flops 6450839040 | bytes 29894656 | tf_op jit(solution)/shard_map/hgts,shd->thgd/dot_general | solution.py:81
  376.6 5.4 %copy.83 = f32[512,2048]{1,0:T(8,128)} copy(f32[512,2048]{0,1:T(8,128)} %bitcast.172) | data formatting | bytes 8388608 | tf_op jit(solution)/shard_map/reshape | solution.py:119
  382.0 32.4 %psum.7 = f32[512]{0:T(512)S(1)} all-reduce(f32[512]{0:T(512)S(1)} %get-tuple-element.21), channel_id=1, replica_groups=mesh['ctx'=64,'head'=2] {'head'}, use_global_device_ids=true, to_apply=%region_13.14 | all-reduce | flops 512 | bytes 4096 | tf_op jit(solution)/shard_map/psum | solution.py:121
  414.5 3.9 fusion.30
  (97 shorter events, 12.8 us)
Async XLA Ops:
  6.5 350.0 %all-gather.4.cloned.1.call-start = ((), (), s32[]{:S(2)}) async-start(), calls=%async_computation | async-start | bytes 8519680 | tf_op jit(solution)/shard_map/all_gather | solution.py:104
  7.2 58.1 %collective-permute-start = (bf16[512]{0:T(512)(128)(2,1)S(1)}, bf16[512]{0:T(512)(128)(2,1)S(1)}, u32[]{:S(2)}, u32[]{:S(2)}) collective-permute-start(bf16[512]{0:T(512)(128)(2,1)S(1)} %convert_element_type.52), channel_id=1, source_target_pairs={{0,8},{2,10},{4,12},{6,14},{8,16},{10,18},{12,20},{14,22},{16,24},... | collective-permute-start | bytes 3080 | tf_op jit(solution)/shard_map/ppermute | solution.py:17
  11.2 58.4 %collective-permute-start.1 = (bf16[512]{0:T(512)(128)(2,1)S(1)}, bf16[512]{0:T(512)(128)(2,1)S(1)}, u32[]{:S(2)}, u32[]{:S(2)}) collective-permute-start(bf16[512]{0:T(512)(128)(2,1)S(1)} %convert_element_type.52), channel_id=1, source_target_pairs={{0,6},{2,8},{4,10},{6,12},{8,14},{10,16},{12,18},{14,20},{16,22},{... | collective-permute-start | bytes 3080 | tf_op jit(solution)/shard_map/ppermute | solution.py:17
  16.8 55.0 %collective-permute-start.2 = (bf16[512]{0:T(512)(128)(2,1)S(1)}, bf16[512]{0:T(512)(128)(2,1)S(1)}, u32[]{:S(2)}, u32[]{:S(2)}) collective-permute-start(bf16[512]{0:T(512)(128)(2,1)S(1)} %convert_element_type.52), channel_id=1, source_target_pairs={{0,4},{2,6},{4,8},{6,10},{8,12},{10,14},{12,16},{14,18},{16,20},{1... | collective-permute-start | bytes 3080 | tf_op jit(solution)/shard_map/ppermute | solution.py:17
  19.3 38.1 %collective-permute-start.3 = (bf16[512]{0:T(512)(128)(2,1)S(1)}, bf16[512]{0:T(512)(128)(2,1)S(1)}, u32[]{:S(2)}, u32[]{:S(2)}) collective-permute-start(bf16[512]{0:T(512)(128)(2,1)S(1)} %convert_element_type.52), channel_id=1, source_target_pairs={{0,2},{2,4},{4,6},{6,8},{8,10},{10,12},{12,14},{14,16},{16,18},{18... | collective-permute-start | bytes 3080 | tf_op jit(solution)/shard_map/ppermute | solution.py:17
  22.3 212.7 %collective-permute-start.4 = (bf16[512,512]{1,0:T(8,128)(2,1)}, bf16[512,512]{1,0:T(8,128)(2,1)}, u32[]{:S(2)}, u32[]{:S(2)}) collective-permute-start(bf16[512,512]{1,0:T(8,128)(2,1)} %param.7), channel_id=1, source_target_pairs={{0,8},{2,10},{4,12},{6,14},{8,16},{10,18},{12,20},{14,22},{16,24},... | collective-permute-start | bytes 1572872 | tf_op jit(solution)/shard_map/ppermute | solution.py:17
  28.5 6.2 %copy-start.16 = (s32[512]{0:T(512)S(1)}, s32[512]{0:T(512)}, u32[]{:S(2)}) copy-start(s32[512]{0:T(512)} %param.10) | copy-start | bytes 6148
  28.5 6.4 %copy-start.18 = (f32[4,512]{1,0:T(4,128)S(1)}, f32[4,512]{1,0:T(4,128)}, u32[]{:S(2)}) copy-start(f32[4,512]{1,0:T(4,128)} %param.9) | copy-start | bytes 24580
  34.6 14.1 %copy-start = (bf16[512,4,4,128]{3,2,1,0:T(4,128)(2,1)}, bf16[512,4,4,128]{3,2,1,0:T(4,128)(2,1)S(1)}, u32[]{:S(2)}) copy-start(bf16[512,4,4,128]{3,2,1,0:T(4,128)(2,1)S(1)} %reshape.272) | copy-start | bytes 6291460
  40.5 8.2 %copy-start.4 = (bf16[512,512]{1,0:T(8,128)(2,1)S(1)}, bf16[512,512]{1,0:T(8,128)(2,1)}, u32[]{:S(2)}) copy-start(bf16[512,512]{1,0:T(8,128)(2,1)} %param.8) | copy-start | bytes 1572868
  48.7 7.5 %copy-start.19 = (u32[128]{0:T(128)S(1)}, u32[128]{0:T(128)}, u32[]{:S(2)}) copy-start(u32[128]{0:T(128)} %constant.42) | copy-start | bytes 1540
  48.7 8.7 %copy-start.5 = (bf16[512,512]{1,0:T(8,128)(2,1)S(1)}, bf16[512,512]{1,0:T(8,128)(2,1)}, u32[]{:S(2)}) copy-start(bf16[512,512]{1,0:T(8,128)(2,1)} %param.7) | copy-start | bytes 1572868
  48.7 5.3 %copy-start.7 = (bf16[512,512]{1,0:T(8,128)(2,1)S(1)}, bf16[512,512]{1,0:T(8,128)(2,1)}, u32[]{:S(2)}) copy-start(bf16[512,512]{1,0:T(8,128)(2,1)} %get-tuple-element.6) | copy-start | bytes 1572868
  48.7 6.3 %copy-start.6 = (bf16[512,512]{1,0:T(8,128)(2,1)S(1)}, bf16[512,512]{1,0:T(8,128)(2,1)}, u32[]{:S(2)}) copy-start(bf16[512,512]{1,0:T(8,128)(2,1)} %get-tuple-element.8) | copy-start | bytes 1572868
  48.8 26.4 %copy-start.11 = (bf16[512,4,128]{0,2,1:T(8,128)(2,1)S(1)}, bf16[512,4,128]{0,2,1:T(8,128)(2,1)}, u32[]{:S(2)}) copy-start(bf16[512,4,128]{0,2,1:T(8,128)(2,1)} %copy.79) | copy-start | bytes 1572868
  57.4 180.7 %collective-permute-start.5 = (bf16[512,512]{1,0:T(8,128)(2,1)S(1)}, bf16[512,512]{1,0:T(8,128)(2,1)}, u32[]{:S(2)}, u32[]{:S(2)}) collective-permute-start(bf16[512,512]{1,0:T(8,128)(2,1)S(1)} %copy-done.5), channel_id=1, source_target_pairs={{0,6},{2,8},{4,10},{6,12},{8,14},{10,16},{12,18},{14,20},{16,22},{... | collective-permute-start | bytes 1572872 | tf_op jit(solution)/shard_map/ppermute | solution.py:17
  65.3 176.0 %collective-permute-start.6 = (bf16[512,512]{1,0:T(8,128)(2,1)S(1)}, bf16[512,512]{1,0:T(8,128)(2,1)}, u32[]{:S(2)}, u32[]{:S(2)}) collective-permute-start(bf16[512,512]{1,0:T(8,128)(2,1)S(1)} %copy-done.5), channel_id=1, source_target_pairs={{0,4},{2,6},{4,8},{6,10},{8,12},{10,14},{12,16},{14,18},{16,20},{1... | collective-permute-start | bytes 1572872 | tf_op jit(solution)/shard_map/ppermute | solution.py:17
  69.6 177.5 %collective-permute-start.7 = (bf16[512,512]{1,0:T(8,128)(2,1)S(1)}, bf16[512,512]{1,0:T(8,128)(2,1)}, u32[]{:S(2)}, u32[]{:S(2)}) collective-permute-start(bf16[512,512]{1,0:T(8,128)(2,1)S(1)} %copy-done.5), channel_id=1, source_target_pairs={{0,2},{2,4},{4,6},{6,8},{8,10},{10,12},{12,14},{14,16},{16,18},{18... | collective-permute-start | bytes 1572872 | tf_op jit(solution)/shard_map/ppermute | solution.py:17
  71.8 192.0 %collective-permute-start.8 = (bf16[512,512]{0,1:T(8,128)(2,1)S(1)}, bf16[512,512]{0,1:T(8,128)(2,1)}, u32[]{:S(2)}, u32[]{:S(2)}) collective-permute-start(bf16[512,512]{0,1:T(8,128)(2,1)S(1)} %copy.55), channel_id=1, source_target_pairs={{0,8},{2,10},{4,12},{6,14},{8,16},{10,18},{12,20},{14,22},{16,24},... | collective-permute-start | bytes 1572872 | tf_op jit(solution)/shard_map/ppermute | solution.py:17
  76.5 173.1 %copy-start.10 = (bf16[512,512]{0,1:T(8,128)(2,1)S(1)}, bf16[512,512]{0,1:T(8,128)(2,1)}, u32[]{:S(2)}) copy-start(bf16[512,512]{0,1:T(8,128)(2,1)} %copy.102) | copy-start | bytes 1572868
  79.2 184.7 %copy-start.8 = (pred[512,2560]{0,1:T(8,128)(4,1)}, pred[512,2560]{0,1:T(8,128)(4,1)S(1)}, u32[]{:S(2)}) copy-start(pred[512,2560]{0,1:T(8,128)(4,1)S(1)} %fusion.29) | copy-start | bytes 3932164
  235.0 29.9 %collective-permute-start.9 = (bf16[512,512]{0,1:T(8,128)(2,1)S(1)}, bf16[512,512]{0,1:T(8,128)(2,1)}, u32[]{:S(2)}, u32[]{:S(2)}) collective-permute-start(bf16[512,512]{0,1:T(8,128)(2,1)S(1)} %copy.55), channel_id=1, source_target_pairs={{0,6},{2,8},{4,10},{6,12},{8,14},{10,16},{12,18},{14,20},{16,22},{... | collective-permute-start | bytes 1572872 | tf_op jit(solution)/shard_map/ppermute | solution.py:17
  238.2 27.9 %collective-permute-start.10 = (bf16[512,512]{0,1:T(8,128)(2,1)S(1)}, bf16[512,512]{0,1:T(8,128)(2,1)}, u32[]{:S(2)}, u32[]{:S(2)}) collective-permute-start(bf16[512,512]{0,1:T(8,128)(2,1)S(1)} %copy.55), channel_id=1, source_target_pairs={{0,4},{2,6},{4,8},{6,10},{8,12},{10,14},{12,16},{14,18},{16,20},{1... | collective-permute-start | bytes 1572872 | tf_op jit(solution)/shard_map/ppermute | solution.py:17
  241.3 25.8 %collective-permute-start.11 = (bf16[512,512]{0,1:T(8,128)(2,1)S(1)}, bf16[512,512]{0,1:T(8,128)(2,1)}, u32[]{:S(2)}, u32[]{:S(2)}) collective-permute-start(bf16[512,512]{0,1:T(8,128)(2,1)S(1)} %copy.55), channel_id=1, source_target_pairs={{0,2},{2,4},{4,6},{6,8},{8,10},{10,12},{12,14},{14,16},{16,18},{18... | collective-permute-start | bytes 1572872 | tf_op jit(solution)/shard_map/ppermute | solution.py:17
  248.2 1.4 copy-start.14
  268.3 9.0 %copy-start.15 = (bf16[2560,512]{0,1:T(8,128)(2,1)}, bf16[2560,512]{0,1:T(8,128)(2,1)S(1)}, u32[]{:S(2)}) copy-start(bf16[2560,512]{0,1:T(8,128)(2,1)S(1)} %constant_dynamic-update-slice_fusion) | copy-start | bytes 7864324
  268.3 9.3 %copy-start.9 = (pred[512,2560]{0,1:T(8,128)(4,1)S(1)}, pred[512,2560]{0,1:T(8,128)(4,1)}, u32[]{:S(2)}) copy-start(pred[512,2560]{0,1:T(8,128)(4,1)} %copy-done.8) | copy-start | bytes 3932164
  344.2 12.3 %copy-start.13 = (f32[64,4]{1,0:T(8,128)S(1)}, f32[64,4]{1,0:T(8,128)}, u32[]{:S(2)}) copy-start(f32[64,4]{1,0:T(8,128)} %pad_select_fusion) | copy-start | bytes 3076
  356.5 5.2 %copy-start.1 = (bf16[512,4,4,128]{3,2,1,0:T(4,128)(2,1)S(1)}, bf16[512,4,4,128]{3,2,1,0:T(4,128)(2,1)}, u32[]{:S(2)}) copy-start(bf16[512,4,4,128]{3,2,1,0:T(4,128)(2,1)} %copy-done) | copy-start | bytes 6291460
  361.8 2.4 copy-start.2
  361.8 2.4 copy-start.3
  361.8 2.4 copy-start.12
  376.6 37.8 %copy-start.17 = (f32[2048]{0:T(1024)S(1)}, f32[2048]{0:T(1024)}, u32[]{:S(2)}) copy-start(f32[2048]{0:T(1024)} %param.11) | copy-start | bytes 24580
Sparse Core Ops, SparseCore 0:
  76.6 89.2 all-gather.3
where the time goes:
time: 434 us; the launch traced here: 426 us
  blocking collectives  187 us (43%)
  matrix products  121 us (28%)
  local copies, waits for them, and re-layouts  41.2 us (9%)
  starting transfers between devices  41.1 us (9%)
  other arithmetic  19.2 us (4%)
  between operations  16.3 us (4%)
    unnamed x1, blocking collectives  155 us
    sub x4, matrix products, body(): exp_scores = jnp.where(allowed, jnp.exp(scores - row_max), 0.0)  58.3 us
    ppermute x12, starting transfers between devices, shifted(): lax.ppermute(value, axis, [(source, source + steps) for source in range(f...  41.1 us
    dot_general x4, matrix products, body(): jnp.einsum('tgk,kd->tgd', weights, v_head, preferred_element_type=jnp.flo...  38.1 us
    psum x1, blocking collectives, body(): sum_total = lax.psum(squares, 'head')  32.4 us
    unnamed x61, local copies, waits for them, and re-layouts  18 us
    dot_general x1, matrix products, body(): jnp.einsum('hgts,shd->thgd', qk_dots * decays[:, None], v_float, precisio...  12.4 us
  transfers between devices with their start and end apart: 13, of which 0 were waited for; matrix products, arithmetic and copies ran while one was open for 35% of the time, Pallas kernels for 0%

commit v1 on v0

v1 whole, which is shorter than its diff:
```python
import math

import jax
import jax.numpy as jnp
from jax import lax
from jax.experimental import pallas as pl
from jax.experimental.pallas import tpu as pltpu
from jax.sharding import PartitionSpec as P

QUERY_HEADS = 32
KEY_VALUE_HEADS = 8
HEAD_SIZE = 128
WINDOW_LENGTH = 2048
LOG2E = 1.4426950408889634
SCALE = LOG2E / math.sqrt(HEAD_SIZE)
HIDDEN = -1e30
SMALL, LARGE = 2.0**-60, 2.0**110
MESH = pl.DeviceIdType.MESH
F32, BF16 = jnp.float32, jnp.bfloat16
T = 512
H = HEAD_SIZE
KV = 4
G = 4
STATE_ROWS = H + 16


def nt(a, b):
    return lax.dot_general(a, b, (((1,), (1,)), ((), ())), preferred_element_type=F32)


def nn(a, b):
    return lax.dot_general(a, b, (((1,), (0,)), ((), ())), preferred_element_type=F32)


def tn(a, b):
    return lax.dot_general(a, b, (((0,), (0,)), ((), ())), preferred_element_type=F32)


def pack_state(state, factor):
    high = factor.astype(BF16).astype(F32)
    middle = (factor - high).astype(BF16).astype(F32)
    low = factor - high - middle
    row = lax.broadcasted_iota(jnp.int32, (16, H), 0)
    tail = jnp.where(row < 4, high, jnp.where(row < 8, middle, low))
    return jnp.concatenate([state, tail], 0).astype(BF16)


def unpack_state(message):
    tail = message[H:, :].astype(F32)
    return message[:H, :].astype(F32), tail[0:1] + tail[4:5] + tail[8:9]


def head_columns(index):
    return pl.ds(pl.multiple_of(index * H, H), H)


def main_kernel(
    q_hbm, k_hbm, v_hbm, decay, ids, gain,
    out_hbm, flag, k_all, v_all, states_in, inverse_out, columns_out, rows_out,
    q, kb, vb, rk, rv, rid, acc, total, lin, causal, later, cum, alive_ref, squares, partner,
    sa, ra, rx, ry, sd, rd, sx, sy, outb, own_decay,
    in_sem, q_sem, out_sem, save_sem, ids_s, ids_r, block_s, block_r,
    st_s, st_r, sq_s, sq_r,
):
    me = lax.axis_index("ctx")
    core = lax.axis_index("head")
    z = lax.rem(me, 4)
    x = lax.rem(me // 4, 4)
    y = me // 16
    line = me - z

    def dev(ctx):
        return {"ctx": ctx, "head": core}

    def around(offset):
        return lax.rem(me + (offset + 64), 64)

    def on_line(position):
        return line + position

    def on_x(position):
        return y * 16 + position * 4 + z

    def on_y(position):
        return position * 16 + x * 4 + z

    def own_chunk(head, kind):
        source, target = ((k_hbm, kb), (v_hbm, vb))[kind]
        return pltpu.make_async_copy(
            source.at[:, pl.ds(head * H, H)], target.at[head], in_sem.at[head, kind]
        )

    chunk_order = (2, 0, 3, 1)
    for head in chunk_order:
        own_chunk(head, 0).start()
        own_chunk(head, 1).start()
    q_copy = pltpu.make_async_copy(q_hbm, q, q_sem)
    q_copy.start()

    barrier = pltpu.get_barrier_semaphore()
    for offset in (1, 2, 3, 4, -1, -2, -3, -4):
        pl.semaphore_signal(barrier, inc=1, device_id=dev(around(offset)), device_id_type=MESH)
    for step in (1, 2, 3):
        for ctx in (
            on_line(lax.rem(z + step, 4)),
            on_x(lax.rem(x + step, 4)),
            on_y(lax.rem(y + step, 4)),
        ):
            pl.semaphore_signal(barrier, inc=1, device_id=dev(ctx), device_id_type=MESH)
    other = {"ctx": me, "head": 1 - core}
    pl.semaphore_signal(barrier, inc=1, device_id=other, device_id_type=MESH)
    pl.semaphore_wait(barrier, 18)

    def id_copy(back):
        return pltpu.make_async_remote_copy(
            src_ref=ids, dst_ref=rid.at[back - 1], send_sem=ids_s.at[back - 1],
            recv_sem=ids_r.at[back - 1], device_id=dev(around(back)), device_id_type=MESH,
        )

    for back in (1, 2, 3, 4):
        id_copy(back).start()

    to_four = around(4)
    to_one = jnp.where(z < 3, around(1), on_line(0))
    to_three = jnp.where(z > 0, around(-1), on_line(3))

    def block_copy(source, back, head, kind, target):
        return pltpu.make_async_remote_copy(
            src_ref=source, dst_ref=(rk, rv)[kind].at[back - 1, head],
            send_sem=block_s.at[back - 1, head, kind], recv_sem=block_r.at[back - 1, head, kind],
            device_id=dev(target), device_id_type=MESH,
        )

    def own_send(step, kind):
        early, late = (step + 2) % 4, step
        block_copy((kb, vb)[kind].at[early], 4, early, kind, to_four).start()

        @pl.when(z < 3)
        def _():
            block_copy((kb, vb)[kind].at[late], 1, late, kind, to_one).start()

        @pl.when(z == 0)
        def _():
            block_copy((kb, vb)[kind].at[early], 3, early, kind, to_three).start()

    def receive(back, head):
        for kind in (0, 1):
            block_copy((kb, vb)[kind].at[head], back, head, kind, to_four).wait_recv()

    def save(back, head):
        for kind in (0, 1):
            pltpu.make_async_copy(
                (rk, rv)[kind].at[back - 1, head], (k_all, v_all)[kind].at[back - 1, head],
                save_sem.at[back - 1, head, kind],
            ).start()

    def relay_four(head):
        receive(4, head)
        for kind in (0, 1):
            held = (rk, rv)[kind].at[3, head]

            @pl.when(z > 0)
            def _():
                block_copy(held, 3, head, kind, to_three).start()

            @pl.when(z == 3)
            def _():
                block_copy(held, 1, head, kind, to_one).start()

        save(4, head)

    def relay_two(head, source_back, target):
        for kind in (0, 1):
            held = (rk, rv)[kind].at[source_back - 1, head]
            block_copy(held, 2, head, kind, target).start()

    for head in chunk_order:
        own_chunk(head, 0).wait()
        own_chunk(head, 1).wait()
        if head == 0:
            own_send(0, 0)
            own_send(0, 1)

    running = decay[...]
    shift = 1
    lane = lax.broadcasted_iota(jnp.int32, (KV, T), 1)
    while shift < T:
        running = running + jnp.where(lane >= shift, pltpu.roll(running, shift, 1), 0.0)
        shift *= 2
    id_row = ids[...].astype(F32)
    rows = jnp.concatenate([running, id_row, jnp.zeros((3, T), F32)], 0)
    rows_out[...] = rows
    columns = jnp.concatenate([rows, jnp.zeros((H - 8, T), F32)], 0).T
    id_column = jnp.broadcast_to(columns[:, 4:5], (T, H))
    for head in range(KV):
        cum[head] = jnp.broadcast_to(columns[:, head : head + 1], (T, H))
    for part in range(4):
        row_at = lax.broadcasted_iota(jnp.int32, (T, H), 0)
        column_at = lax.broadcasted_iota(jnp.int32, (T, H), 1) + part * H
        span = slice(part * H, (part + 1) * H)
        linked = (column_at <= row_at) & (id_column == id_row[:, span])
        causal[:, span] = jnp.where(linked, 0.0, HIDDEN)
        later[:, span] = jnp.where(column_at > row_at, 0.0, HIDDEN)
    last_id = id_row[:, T - 1 : T]
    own_tail = id_column == last_id

    for back in (1, 2, 3, 4):
        id_copy(back).wait_recv()
    prev_id = jnp.where(me > 0, rid[0].astype(F32)[:, T - 1 : T], -1.0)
    before = jnp.zeros((1, 1), F32)
    for back in (1, 2, 3, 4):
        same = (rid[back - 1].astype(F32) == prev_id).astype(F32)
        count = jnp.sum(same, axis=1, keepdims=True)
        before = before + jnp.where(me >= back, count, 0.0)
    alive = (id_column == prev_id).astype(F32)
    alive_ref[...] = alive
    lane_at = lax.broadcasted_iota(jnp.int32, (T, H), 1)
    columns_out[...] = jnp.where(
        lane_at == 5, alive, jnp.where(lane_at == 6, jnp.broadcast_to(before, (T, H)), columns)
    )
    own_carry = (last_id == prev_id).astype(F32)

    for head in range(KV):
        end = running[head : head + 1, T - 1 : T]
        weight = jnp.where(own_tail, jnp.exp(end - cum[head]), 0.0)
        weighted = (kb[head].astype(F32) * weight).astype(BF16)
        state = tn(weighted, vb[head])
        factor = jnp.broadcast_to(jnp.exp(end) * own_carry, (1, H))
        sa[head] = pack_state(state, factor)

    def state_copy(stage, source, target, slot, ctx):
        return pltpu.make_async_remote_copy(
            src_ref=source, dst_ref=target.at[slot], send_sem=st_s.at[stage, slot],
            recv_sem=st_r.at[stage, slot], device_id=dev(ctx), device_id_type=MESH,
        )

    def state_send(stage, step):
        if stage == 0:
            to = lax.rem(z + step, 4)
            return pltpu.make_async_remote_copy(
                src_ref=sa.at[to], dst_ref=ra.at[z], send_sem=st_s.at[0, step], recv_sem=st_r.at[0, step],
                device_id=dev(on_line(to)), device_id_type=MESH,
            )
        if stage == 1:
            return pltpu.make_async_remote_copy(
                src_ref=sx, dst_ref=rx.at[x], send_sem=st_s.at[1, step], recv_sem=st_r.at[1, step],
                device_id=dev(on_x(lax.rem(x + step, 4))), device_id_type=MESH,
            )
        if stage == 2:
            return pltpu.make_async_remote_copy(
                src_ref=sy, dst_ref=ry.at[y], send_sem=st_s.at[2, step], recv_sem=st_r.at[2, step],
                device_id=dev(on_y(lax.rem(y + step, 4))), device_id_type=MESH,
            )
        to = lax.rem(z + step, 4)
        return pltpu.make_async_remote_copy(
            src_ref=sd.at[to], dst_ref=rd.at[z], send_sem=st_s.at[3, step], recv_sem=st_r.at[3, step],
            device_id=dev(on_line(to)), device_id_type=MESH,
        )

    def start_stage(stage):
        for step in (1, 2, 3):
            state_send(stage, step).start()

    def finish_stage(stage):
        for step in (1, 2, 3):
            state_send(stage, step).wait_recv()

    ra[z] = sa[z]
    start_stage(0)

    def fold(messages, limit=None):
        state, factor = jnp.zeros((H, H), F32), jnp.ones((1, H), F32)
        for position in range(4):
            item, by = unpack_state(messages[position])
            fresh, grown = state * by + item, factor * by
            if limit is None:
                state, factor = fresh, grown
            else:
                state = jnp.where(position < limit, fresh, state)
        return state, factor

    def after_line():
        finish_stage(0)
        sx[...] = pack_state(*fold(ra))
        rx[x] = sx[...]
        start_stage(1)

    def after_x():
        finish_stage(1)
        sy[...] = pack_state(*fold(rx))
        ry[y] = sy[...]
        start_stage(2)

    def after_y():
        finish_stage(2)
        state, _ = fold(ry, y)
        for position in range(4):
            item, by = unpack_state(rx[position])
            state = jnp.where(position < x, state * by + item, state)
        for position in range(4):
            sd[position] = state.astype(BF16)
            item, by = unpack_state(ra[position])
            state = state * by + item
        rd[z] = sd[z]
        start_stage(3)

    q_copy.wait()

    def own_unit(head):
        keys, values = kb[head], vb[head]
        wide = jnp.concatenate([values, jnp.ones((T, H), BF16)], 1)
        row = rows_out[pl.ds(head, 1), :]
        for first in (0, 256):
            here, upto = slice(first, first + 256), first + 256
            column = cum[head, here, :]
            for part in range(0, upto, H):
                span = slice(part, part + H)
                own_decay[here, span] = jnp.exp(column - row[:, span] + causal[here, span])
        for first in (0, 256):
            here, upto = slice(first, first + 256), first + 256
            for member in range(G):
                at = head_columns(head * G + member)
                scores = nt(q[here, at], keys[:upto])
                grown = jnp.exp2(scores * SCALE + causal[here, :upto]).astype(BF16)
                mixed = nn(grown, wide[:upto])
                acc[here, at] = mixed[:, :H]
                total[here, at] = mixed[:, H:]
                lin[here, at] = nn((scores * own_decay[here, :upto]).astype(BF16), values[:upto])

    def masked_values(back, head):
        place = lax.broadcasted_iota(jnp.int32, (T, H), 0).astype(F32)
        kept = place >= back * float(T) - columns_out[0:1, 6:7]
        values = jnp.where(kept, rv[back - 1, head].astype(F32), 0.0)
        return jnp.concatenate([values, jnp.where(kept, 1.0, 0.0)], 1).astype(BF16)

    def gather(here, at, mixed):
        live = alive_ref[here, :] > 0.0
        acc[here, at] += jnp.where(live, mixed[:, :H], 0.0)
        total[here, at] += jnp.where(live, mixed[:, H:], 0.0)

    def far_unit(back, head):
        keys, wide = rk[back - 1, head], masked_values(back, head)
        for member in range(G):
            at = head_columns(head * G + member)
            grown = jnp.exp2(nt(q[:, at], keys) * SCALE).astype(BF16)
            gather(slice(0, T), at, nn(grown, wide))

    def oldest_unit(head):
        keys, wide = rk[3, head], masked_values(4, head)
        for first in (0, 256):
            here, since = slice(first, first + 256), slice(first, T)
            for member in range(G):
                at = head_columns(head * G + member)
                scores = nt(q[here, at], keys[since])
                grown = jnp.exp2(scores * SCALE + later[here, since]).astype(BF16)
                gather(here, at, nn(grown, wide[since]))

    own_send(1, 0)

    def own_step(head, carry):
        own_unit(head)

        @pl.when(head == 0)
        def _():
            own_send(1, 1)

        @pl.when(head == 1)
        def _():
            own_send(2, 0)
            after_line()
            relay_four(2)

        @pl.when(head == 2)
        def _():
            own_send(2, 1)

        @pl.when(head == 3)
        def _():
            own_send(3, 0)
            own_send(3, 1)
            relay_four(3)
            after_x()

        return carry

    lax.fori_loop(0, KV, own_step, 0)

    def near_step(step, carry):
        early = lax.rem(step + 2, 4)

        @pl.when(step >= 2)
        def _():
            relay_four(early)

        oldest_unit(early)
        receive(1, step)
        save(1, step)

        @pl.when(step < 2)
        def _():
            relay_two(step, 1, around(1))

        @pl.when(step >= 2)
        def _():
            receive(3, step)
            save(3, step)
            relay_two(step, 3, around(-1))

        @pl.when(step == 1)
        def _():
            after_y()

        far_unit(1, step)
        return carry

    lax.fori_loop(0, KV, near_step, 0)

    def cross():
        finish_stage(3)
        squares[...] = jnp.zeros((T, H), F32)

        def cross_step(head, carry):
            state = rd[head]
            states_in[head] = state.astype(F32)
            entry = jnp.exp(cum[head]) * alive_ref[...]
            part = squares[...]
            for member in range(G):
                at = head_columns(head * G + member)
                whole = lin[:, at] + nn(q[:, at], state) * entry
                lin[:, at] = whole
                part = part + whole * whole
            squares[...] = part
            return carry

        lax.fori_loop(0, KV, cross_step, 0)
        row_sum = jnp.sum(squares[...], axis=1, keepdims=True)
        squares[...] = jnp.broadcast_to(row_sum, (T, H))
        square_copy().start()

    def square_copy():
        return pltpu.make_async_remote_copy(
            src_ref=squares, dst_ref=partner, send_sem=sq_s, recv_sem=sq_r, device_id=other,
            device_id_type=MESH,
        )

    def out_copy(head):
        wide = pl.ds(pl.multiple_of(head * G * H, G * H), G * H)
        return pltpu.make_async_copy(outb.at[:, wide], out_hbm.at[:, wide], out_sem.at[head])

    def far_step(step, carry):
        back = jnp.where(step < 4, 3, 2)
        head = jnp.where(step < 4, lax.rem(step + 2, 4), lax.rem(step, 4))

        @pl.when((step == 2) | (step == 3))
        def _():
            receive(3, head)
            save(3, head)

        @pl.when(step == 4)
        def _():
            cross()

        @pl.when(step >= 4)
        def _():
            receive(2, head)
            save(2, head)

        @pl.when(step == 5)
        def _():
            square_copy().wait_recv()
            mean = (squares[...] + partner[...]) * (1.0 / (QUERY_HEADS * HEAD_SIZE))
            inverse_out[...] = lax.rsqrt(mean + 1e-06)
            flag[...] = jnp.zeros((8, H), F32)

        far_unit(back, head)

        return carry

    lax.fori_loop(0, 8, far_step, 0)

    def last_step(head, carry):
        for member in range(G):
            at = head_columns(head * G + member)
            mass = total[:, at]
            good = (mass >= SMALL) & (mass <= LARGE)
            flag[...] += jnp.sum(jnp.where(good, 0.0, 1.0).reshape(T // 8, 8, H), axis=0)
            mixed = acc[:, at] / mass + gain[:, at] * (lin[:, at] * inverse_out[...])
            outb[:, at] = mixed.astype(BF16)
        out_copy(head).start()
        return carry

    lax.fori_loop(0, KV, last_step, 0)

    for head in range(KV):
        out_copy(head).wait()
        for kind in (0, 1):
            for back in (1, 2, 3, 4):
                held = (rk, rv)[kind].at[back - 1, head]
                pltpu.make_async_copy(
                    held, (k_all, v_all)[kind].at[back - 1, head], save_sem.at[back - 1, head, kind]
                ).wait()
                block_copy(held, back, head, kind, to_four).wait_send()
    for back in (1, 2, 3, 4):
        id_copy(back).wait_send()
    for stage in range(4):
        for step in (1, 2, 3):
            state_send(stage, step).wait_send()
    square_copy().wait_send()


def finish_kernel(
    flag, cand, q_hbm, k_hbm, v_hbm, k_all, v_all, states_hbm, inverse_hbm, columns_hbm, rows_hbm, gain_hbm,
    out_hbm, q, ks, vs, outb, states_in, inverse, columns, rows, gain, sems,
):
    bad = jnp.max(flag[...]) > 0.0

    @pl.when(jnp.logical_not(bad))
    def _():
        pieces = [pl.ds(part * (T // 8), T // 8) for part in range(8)]
        arrive = [
            pltpu.make_async_copy(cand.at[piece], outb.at[piece], sems.at[part])
            for part, piece in enumerate(pieces)
        ]
        leave = [
            pltpu.make_async_copy(outb.at[piece], out_hbm.at[piece], sems.at[part])
            for part, piece in enumerate(pieces)
        ]
        for copy in arrive:
            copy.start()
        for there, onward in zip(arrive, leave):
            there.wait()
            onward.start()
        for copy in leave:
            copy.wait()

    @pl.when(bad)
    def _():
        def bring(source, target, sem):
            copy = pltpu.make_async_copy(source, target, sems.at[sem])
            copy.start()
            copy.wait()

        bring(q_hbm, q, 0)
        bring(states_hbm, states_in, 0)
        bring(inverse_hbm, inverse, 0)
        bring(columns_hbm, columns, 0)
        bring(rows_hbm, rows, 0)
        bring(gain_hbm, gain, 0)
        for head in range(KV):
            for source, whole, target in ((k_hbm, k_all, ks), (v_hbm, v_all, vs)):
                bring(source.at[:, pl.ds(head * H, H)], target.at[head, pl.ds(4 * T, T)], 0)
                for back in (1, 2, 3, 4):
                    bring(whole.at[back - 1, head], target.at[head, pl.ds((4 - back) * T, T)], 0)

        def query_step(index, carry):
            head = index // G
            at = head_columns(index)
            for first in range(0, T, 128):
                here = pl.ds(first, 128)
                queries = q[here, at]
                id_column, alive = columns[here, 4:5], columns[here, 5:6]
                before = columns[here, 6:7]
                spot = lax.broadcasted_iota(jnp.int32, (128, 5 * T), 1)
                turn = lax.broadcasted_iota(jnp.int32, (128, 5 * T), 0) + first
                inside = (spot > turn) & (spot <= turn + 4 * T)
                ids = jnp.concatenate([jnp.zeros((1, 4 * T), F32), rows[4:5, :]], 1)
                old = (alive > 0.0) & (spot.astype(F32) >= 4.0 * T - before)
                allowed = inside & (((spot < 4 * T) & old) | ((spot >= 4 * T) & (ids == id_column)))
                scores = nt(queries, ks[head]) * (1.0 / math.sqrt(HEAD_SIZE))
                scores = jnp.where(allowed, scores, HIDDEN)
                top = jnp.max(scores, axis=1, keepdims=True)
                grown = jnp.where(allowed, jnp.exp(scores - top), 0.0)
                weights = grown / jnp.sum(grown, axis=1, keepdims=True)
                window = nn(weights.astype(BF16), vs[head])
                row = rows[pl.ds(head, 1), :]
                lane = lax.broadcasted_iota(jnp.int32, (128, H), 1)
                column = jnp.sum(
                    jnp.where(lane == head, columns[here, :], 0.0), axis=1, keepdims=True
                )
                own_at = lax.broadcasted_iota(jnp.int32, (128, T), 1)
                own_turn = lax.broadcasted_iota(jnp.int32, (128, T), 0) + first
                linked = (own_at <= own_turn) & (rows[4:5, :] == id_column)
                gap = jnp.where(linked, column - row, 0.0)
                kept = jnp.where(linked, jnp.exp(gap), 0.0)
                dots = nt(queries, ks[head, pl.ds(4 * T, T)]) * kept
                linear = nn(dots.astype(BF16), vs[head, pl.ds(4 * T, T)])
                entry = jnp.exp(column) * alive
                linear = linear + nn(queries, states_in[head].astype(BF16)) * entry
                mixed = window + gain[:, at] * (linear * inverse[here, :])
                outb[here, at] = mixed.astype(BF16)
            return carry

        lax.fori_loop(0, KV * G, query_step, 0)
        bring(outb, out_hbm, 0)


def body(queries, keys, values, token_log_decay, seq_ids, norm_gain):
    any_spec = pl.BlockSpec(memory_space=pltpu.HBM)
    vmem_spec = pl.BlockSpec(memory_space=pltpu.VMEM)
    dma = pltpu.SemaphoreType.DMA
    gain = norm_gain.reshape(1, -1)
    ids = seq_ids.reshape(1, -1)
    wide = KV * G * H
    results = pl.pallas_call(
        main_kernel,
        out_shape=(
            jax.ShapeDtypeStruct((T, wide), BF16),
            jax.ShapeDtypeStruct((8, H), F32),
            jax.ShapeDtypeStruct((4, KV, T, H), BF16),
            jax.ShapeDtypeStruct((4, KV, T, H), BF16),
            jax.ShapeDtypeStruct((KV, H, H), F32),
            jax.ShapeDtypeStruct((T, H), F32),
            jax.ShapeDtypeStruct((T, H), F32),
            jax.ShapeDtypeStruct((8, T), F32),
        ),
        in_specs=[any_spec] * 3 + [vmem_spec] * 3,
        out_specs=(any_spec, vmem_spec, any_spec, any_spec, vmem_spec, vmem_spec, vmem_spec, vmem_spec),
        scratch_shapes=[
            pltpu.VMEM((T, wide), BF16),
            pltpu.VMEM((KV, T, H), BF16),
            pltpu.VMEM((KV, T, H), BF16),
            pltpu.VMEM((4, KV, T, H), BF16),
            pltpu.VMEM((4, KV, T, H), BF16),
            pltpu.VMEM((4, 1, T), jnp.int32),
            pltpu.VMEM((T, wide), F32),
            pltpu.VMEM((T, wide), F32),
            pltpu.VMEM((T, wide), F32),
            pltpu.VMEM((T, T), F32),
            pltpu.VMEM((T, T), F32),
            pltpu.VMEM((KV, T, H), F32),
            pltpu.VMEM((T, H), F32),
            pltpu.VMEM((T, H), F32),
            pltpu.VMEM((T, H), F32),
            pltpu.VMEM((4, STATE_ROWS, H), BF16),
            pltpu.VMEM((4, STATE_ROWS, H), BF16),
            pltpu.VMEM((4, STATE_ROWS, H), BF16),
            pltpu.VMEM((4, STATE_ROWS, H), BF16),
            pltpu.VMEM((4, H, H), BF16),
            pltpu.VMEM((4, H, H), BF16),
            pltpu.VMEM((STATE_ROWS, H), BF16),
            pltpu.VMEM((STATE_ROWS, H), BF16),
            pltpu.VMEM((T, wide), BF16),
            pltpu.VMEM((T, T), F32),
            dma((KV, 2)),
            dma,
            dma((KV,)),
            dma((4, KV, 2)),
            dma((4,)),
            dma((4,)),
            dma((4, KV, 2)),
            dma((4, KV, 2)),
            dma((4, 4)),
            dma((4, 4)),
            dma,
            dma,
        ],
        compiler_params=pltpu.CompilerParams(
            collective_id=0, has_side_effects=True, vmem_limit_bytes=56 << 20
        ),
        name="attend",
    )(queries, keys, values, token_log_decay, ids, gain)
    cand, flag, k_all, v_all, states_in, inverse, columns, rows = results
    return pl.pallas_call(
        finish_kernel,
        out_shape=jax.ShapeDtypeStruct((T, wide), BF16),
        in_specs=[vmem_spec] + [any_spec] * 11,
        out_specs=any_spec,
        scratch_shapes=[
            pltpu.VMEM((T, wide), BF16),
            pltpu.VMEM((KV, 5 * T, H), BF16),
            pltpu.VMEM((KV, 5 * T, H), BF16),
            pltpu.VMEM((T, wide), BF16),
            pltpu.VMEM((KV, H, H), F32),
            pltpu.VMEM((T, H), F32),
            pltpu.VMEM((T, H), F32),
            pltpu.VMEM((8, T), F32),
            pltpu.VMEM((1, wide), F32),
            dma((8,)),
        ],
        compiler_params=pltpu.CompilerParams(vmem_limit_bytes=56 << 20),
        name="finish",
    )(flag, cand, queries, keys, values, k_all, v_all, states_in, inverse, columns, rows, gain)


def solution(mesh):
    return jax.shard_map(
        body,
        mesh=mesh,
        in_specs=(
            P("ctx", "head"),
            P("ctx", "head"),
            P("ctx", "head"),
            P("head", "ctx"),
            P("ctx"),
            P("head"),
        ),
        out_specs=P("ctx", "head"),
        check_vma=False,
    )
```

time: 434 us -> 207 us (0.48); the launches traced: 426 us -> 206 us
  Pallas kernels: 0 us -> 205 us
  blocking collectives: 187 us -> 0 us
  matrix products: 121 us -> 0 us
  local copies, waits for them, and re-layouts: 41.2 us -> 0 us
  starting transfers between devices: 41.1 us -> 0 us
  other arithmetic: 19.2 us -> 0 us
  between operations: 16.3 us -> 0.17 us
    pallas_call x0 -> x2, Pallas kernels: none -> 205 us  [the longest x1 116 us: body(): pl.pallas_call(finish_kernel, out_shape=jax.ShapeDtypeStruct((T, wide), B...]
    unnamed x1 -> x0, blocking collectives: 155 us -> none
    dot_general x8 -> x0, matrix products: 62.4 us -> none  [the longest x4 38.1 us: body(): jnp.einsum('tgk,kd->tgd', weights, v_head, preferred_element_type=jnp.flo...]
    sub x4 -> x0, matrix products: 58.3 us -> none  [body(): exp_scores = jnp.where(allowed, jnp.exp(scores - row_max), 0.0)]
    ppermute x12 -> x0, starting transfers between devices: 41.1 us -> none  [shifted(): lax.ppermute(value, axis, [(source, source + steps) for source in range(f...]
    psum x1 -> x0, blocking collectives: 32.4 us -> none  [body(): sum_total = lax.psum(squares, 'head')]
    unnamed x61 -> x0, local copies, waits for them, and re-layouts: 18 us -> none
    reshape x10 -> x0, local copies, waits for them, and re-layouts: 17.9 us -> none  [the longest x4 6.07 us: body(): head_outputs.append(head_out.reshape(tok_rows, query_groups * HEAD_SIZE))]
  transfers between devices with their start and end apart: 13 -> 0, of which waited for: 0 -> 0; matrix products, arithmetic and copies ran while one was open for 35% -> 0% of each run, Pallas kernels for 0% -> 0%
where the time goes in v1:
time: 207 us; the launch traced here: 206 us
  Pallas kernels  205 us (99%)
    pallas_call x1, Pallas kernels, body(): pl.pallas_call(finish_kernel, out_shape=jax.ShapeDtypeStruct((T, wide), B...  116 us
    pallas_call x1, Pallas kernels, body(): pl.pallas_call(main_kernel, out_shape=(jax.ShapeDtypeStruct((T, wide), BF...  89.9 us

profile of v1, /device:TPU:1, one launch (start us, length us, event | category | flops | bytes accessed | tf_op | source)
XLA Modules:
  0.0 205.6 jit_solution(9715455609645680093)
XLA Ops:
  0.0 89.9 %attend.1 = (bf16[512,2048]{1,0:T(8,128)(2,1)}, f32[8,128]{1,0:T(8,128)}, bf16[4,4,512,128]{3,2,1,0:T(8,128)(2,1)}, bf16[4,4,512,128]{3,2,1,0:T(8,128)(2,1)}, f3...) custom-call(bf16[512,2048]{1,0:T(8,128)(2,1)} %q_hbm.3, ...), custom_call_target="tpu_custom_call" | custom-call | tf_op jit(solution)/shard_map/attend/pallas_call | solution.py:604
  89.9 115.6 %finish.1 = bf16[512,2048]{1,0:T(8,128)(2,1)} custom-call(f32[8,128]{1,0:T(8,128)} %get-tuple-element.13.flag, bf16[512,2048]{1,0:T(8,128)(2,1)} %get-tuple-element.14.cand, bf16[512,2048]{1,0:T(8,128)(2,1)} %q_hbm.3, bf16[512,512]{1,0:T(8,128)(2,1)} %k_hbm.3, bf16[512,512]{1,0:T(8,128)(2,1)} %v_hbm.3, bf16[4,4,512,128]{3,2,1,0:T(8,128)(2,1)} %get-tuple-element.15.k_all, ...), custom_call_target="tpu_custom_call" | custom-call | tf_op jit(solution)/shard_map/finish/pallas_call | solution.py:663

commit v2 on v1

--- a/solution.py
+++ b/solution.py
@@ -22,6 +22,12 @@
 KV = 4
 G = 4
 STATE_ROWS = H + 16
+ORDERS = (
+    ((1, 0), (3, 2), (3, 3), (1, 1), (3, 0), (3, 1), (2, 0), (1, 2), (2, 1), (2, 2), (1, 3), (2, 3)),
+    ((1, 0), (1, 1), (3, 2), (1, 2), (3, 3), (1, 3), (3, 0), (3, 1), (2, 0), (2, 1), (2, 2), (2, 3)),
+    ((1, 0), (1, 1), (3, 0), (1, 2), (3, 1), (3, 2), (1, 3), (3, 3), (2, 0), (2, 1), (2, 2), (2, 3)),
+    ((1, 0), (3, 2), (1, 1), (3, 3), (1, 2), (3, 0), (1, 3), (3, 1), (2, 0), (2, 1), (2, 2), (2, 3)),
+)
 
 
 def nt(a, b):
@@ -59,8 +65,9 @@
     out_hbm, flag, k_all, v_all, states_in, inverse_out, columns_out, rows_out,
     q, kb, vb, rk, rv, rid, acc, total, lin, causal, later, cum, alive_ref, squares, partner,
     sa, ra, rx, ry, sd, rd, sx, sy, outb, own_decay,
+    sk, sv,
     in_sem, q_sem, out_sem, save_sem, ids_s, ids_r, block_s, block_r,
-    st_s, st_r, sq_s, sq_r,
+    st_s, st_r, sq_s, sq_r, stop_s, stop_r,
 ):
     me = lax.axis_index("ctx")
     core = lax.axis_index("head")
@@ -131,8 +138,13 @@
             device_id=dev(target), device_id_type=MESH,
         )
 
+    first_early = jnp.where(z < 3, 2, 0)
+
+    def early_head(step):
+        return lax.rem(first_early + step, 4)
+
     def own_send(step, kind):
-        early, late = (step + 2) % 4, step
+        early, late = early_head(step), step
         block_copy((kb, vb)[kind].at[early], 4, early, kind, to_four).start()
 
         @pl.when(z < 3)
@@ -154,25 +166,71 @@
                 save_sem.at[back - 1, head, kind],
             ).start()
 
-    def relay_four(head):
+    def relay_four(step):
+        head = early_head(step)
         receive(4, head)
         for kind in (0, 1):
             held = (rk, rv)[kind].at[3, head]
 
+            @pl.when(z == 3)
+            def _():
+                block_copy(held, 1, head, kind, to_one).start()
+
             @pl.when(z > 0)
             def _():
                 block_copy(held, 3, head, kind, to_three).start()
 
+        save(4, head)
+
+    def stop_copy(source, head, kind, target):
+        slot = lax.rem(head, 2)
+        return pltpu.make_async_remote_copy(
+            src_ref=source, dst_ref=(sk, sv)[kind].at[slot],
+            send_sem=block_s.at[1, head, kind], recv_sem=stop_r.at[slot, kind],
+            device_id=dev(target), device_id_type=MESH,
+        )
+
+    def relay_up(head):
+        for kind in (0, 1):
+            held = (rk, rv)[kind].at[0, head]
+
+            @pl.when(z < 3)
+            def _():
+                block_copy(held, 2, head, kind, around(1)).start()
+
             @pl.when(z == 3)
             def _():
-                block_copy(held, 1, head, kind, to_one).start()
-
-        save(4, head)
-
-    def relay_two(head, source_back, target):
+                stop_copy(held, head, kind, on_line(0)).start()
+
+    def relay_down(head):
         for kind in (0, 1):
-            held = (rk, rv)[kind].at[source_back - 1, head]
-            block_copy(held, 2, head, kind, target).start()
+            held = (rk, rv)[kind].at[2, head]
+
+            @pl.when(z > 0)
+            def _():
+                block_copy(held, 2, head, kind, around(-1)).start()
+
+            @pl.when(z == 0)
+            def _():
+                stop_copy(held, head, kind, on_line(3)).start()
+
+    onward_line = jnp.where(z == 0, around(4), around(-4))
+    onward_first = jnp.where(z == 0, 0, 2)
+
+    def onward_copy(slot, kind):
+        head = onward_first + slot
+        return pltpu.make_async_remote_copy(
+            src_ref=(sk, sv)[kind].at[slot], dst_ref=(rk, rv)[kind].at[1, head],
+            send_sem=stop_s.at[slot, kind], recv_sem=block_r.at[1, head, kind],
+            device_id=dev(onward_line), device_id_type=MESH,
+        )
+
+    def hand_on(slot, at):
+        @pl.when(z == at)
+        def _():
+            for kind in (0, 1):
+                stop_copy((sk, sv)[kind].at[slot], slot, kind, on_line(0)).wait_recv()
+                onward_copy(slot, kind).start()
 
     for head in chunk_order:
         own_chunk(head, 0).wait()
@@ -180,6 +238,7 @@
         if head == 0:
             own_send(0, 0)
             own_send(0, 1)
+    own_send(1, 0)
 
     running = decay[...]
     shift = 1
@@ -355,65 +414,36 @@
                 grown = jnp.exp2(scores * SCALE + later[here, since]).astype(BF16)
                 gather(here, at, nn(grown, wide[since]))
 
-    own_send(1, 0)
+    relay_four(0)
+    own_send(1, 1)
 
     def own_step(head, carry):
         own_unit(head)
 
         @pl.when(head == 0)
         def _():
-            own_send(1, 1)
+            own_send(2, 0)
 
         @pl.when(head == 1)
         def _():
-            own_send(2, 0)
             after_line()
-            relay_four(2)
+            own_send(2, 1)
 
         @pl.when(head == 2)
         def _():
-            own_send(2, 1)
+            relay_four(1)
+            own_send(3, 0)
 
         @pl.when(head == 3)
         def _():
-            own_send(3, 0)
             own_send(3, 1)
-            relay_four(3)
-            after_x()
+            receive(1, 0)
+            relay_up(0)
+            save(1, 0)
 
         return carry
 
     lax.fori_loop(0, KV, own_step, 0)
-
-    def near_step(step, carry):
-        early = lax.rem(step + 2, 4)
-
-        @pl.when(step >= 2)
-        def _():
-            relay_four(early)
-
-        oldest_unit(early)
-        receive(1, step)
-        save(1, step)
-
-        @pl.when(step < 2)
-        def _():
-            relay_two(step, 1, around(1))
-
-        @pl.when(step >= 2)
-        def _():
-            receive(3, step)
-            save(3, step)
-            relay_two(step, 3, around(-1))
-
-        @pl.when(step == 1)
-        def _():
-            after_y()
-
-        far_unit(1, step)
-        return carry
-
-    lax.fori_loop(0, KV, near_step, 0)
 
     def cross():
         finish_stage(3)
@@ -447,38 +477,73 @@
         wide = pl.ds(pl.multiple_of(head * G * H, G * H), G * H)
         return pltpu.make_async_copy(outb.at[:, wide], out_hbm.at[:, wide], out_sem.at[head])
 
+    def listed(step):
+        code = jnp.int32(0)
+        for place, order in enumerate(ORDERS):
+            mine = jnp.int32(0)
+            for index, (back, head) in enumerate(order):
+                mine = jnp.where(step == index, back * 4 + head, mine)
+            code = jnp.where(z == place, mine, code)
+        return code // 4, lax.rem(code, 4)
+
     def far_step(step, carry):
-        back = jnp.where(step < 4, 3, 2)
-        head = jnp.where(step < 4, lax.rem(step + 2, 4), lax.rem(step, 4))
-
-        @pl.when((step == 2) | (step == 3))
-        def _():
-            receive(3, head)
-            save(3, head)
-
-        @pl.when(step == 4)
-        def _():
+        back, head = listed(step)
+
+        @pl.when(step == 0)
+        def _():
+            after_x()
+
+        @pl.when(step == 1)
+        def _():
+            relay_four(2)
+
+        @pl.when(step == 2)
+        def _():
+            after_y()
+            hand_on(0, 0)
+
+        @pl.when(step == 3)
+        def _():
+            relay_four(3)
+
+        @pl.when(step == 6)
+        def _():
+            hand_on(1, 0)
+            hand_on(0, 3)
             cross()
 
-        @pl.when(step >= 4)
-        def _():
-            receive(2, head)
-            save(2, head)
-
-        @pl.when(step == 5)
-        def _():
+        @pl.when(step == 8)
+        def _():
+            hand_on(1, 3)
             square_copy().wait_recv()
             mean = (squares[...] + partner[...]) * (1.0 / (QUERY_HEADS * HEAD_SIZE))
             inverse_out[...] = lax.rsqrt(mean + 1e-06)
             flag[...] = jnp.zeros((8, H), F32)
 
+        @pl.when((back != 1) | (head != 0))
+        def _():
+            receive(back, head)
+            save(back, head)
+
+        @pl.when((back == 1) & (head == 1))
+        def _():
+            relay_up(head)
+
+        @pl.when((back == 3) & (head >= 2))
+        def _():
+            relay_down(head)
+
         far_unit(back, head)
-
         return carry
 
-    lax.fori_loop(0, 8, far_step, 0)
-
-    def last_step(head, carry):
+    def old_step(step, carry):
+        oldest_unit(early_head(step))
+        lax.fori_loop(2 * step, 2 * step + 2, far_step, 0)
+        return carry
+
+    def last_step(step, carry):
+        far_step(step, carry)
+        head = step - 8
         for member in range(G):
             at = head_columns(head * G + member)
             mass = total[:, at]
@@ -489,7 +554,8 @@
         out_copy(head).start()
         return carry
 
-    lax.fori_loop(0, KV, last_step, 0)
+    lax.fori_loop(0, 4, old_step, 0)
+    lax.fori_loop(8, 12, last_step, 0)
 
     for head in range(KV):
         out_copy(head).wait()
@@ -506,6 +572,12 @@
         for step in (1, 2, 3):
             state_send(stage, step).wait_send()
     square_copy().wait_send()
+
+    @pl.when((z == 0) | (z == 3))
+    def _():
+        for slot in (0, 1):
+            for kind in (0, 1):
+                onward_copy(slot, kind).wait_send()
 
 
 def finish_kernel(
@@ -641,6 +713,8 @@
             pltpu.VMEM((STATE_ROWS, H), BF16),
             pltpu.VMEM((T, wide), BF16),
             pltpu.VMEM((T, T), F32),
+            pltpu.VMEM((2, T, H), BF16),
+            pltpu.VMEM((2, T, H), BF16),
             dma((KV, 2)),
             dma,
             dma((KV,)),
@@ -653,6 +727,8 @@
             dma((4, 4)),
             dma,
             dma,
+            dma((2, 2)),
+            dma((2, 2)),
         ],
         compiler_params=pltpu.CompilerParams(
             collective_id=0, has_side_effects=True, vmem_limit_bytes=56 << 20

time: 207 us -> 189 us (0.913)
  Pallas kernels: 205 us -> 187 us
    pallas_call x1, Pallas kernels: 89.9 us -> 71.8 us  [body(): pl.pallas_call(main_kernel, out_shape=(jax.ShapeDtypeStruct((T, wide), BF...]
where the time goes in v2:
time: 189 us; the launch traced here: 188 us
  Pallas kernels  187 us (99%)
    pallas_call x1, Pallas kernels, body(): pl.pallas_call(finish_kernel, out_shape=jax.ShapeDtypeStruct((T, wide), B...  116 us
    pallas_call x1, Pallas kernels, body(): pl.pallas_call(main_kernel, out_shape=(jax.ShapeDtypeStruct((T, wide), BF...  71.8 us

profile of v2, /device:TPU:1, one launch (start us, length us, event | category | flops | bytes accessed | tf_op | source)
XLA Modules:
  0.0 187.5 jit_solution(7116197798639465170)
XLA Ops:
  0.0 71.8 %attend.1 = (bf16[512,2048]{1,0:T(8,128)(2,1)}, f32[8,128]{1,0:T(8,128)}, bf16[4,4,512,128]{3,2,1,0:T(8,128)(2,1)}, bf16[4,4,512,128]{3,2,1,0:T(8,128)(2,1)}, f3...) custom-call(bf16[512,2048]{1,0:T(8,128)(2,1)} %q_hbm.3, ...), custom_call_target="tpu_custom_call" | custom-call | tf_op jit(solution)/shard_map/attend/pallas_call | solution.py:676
  71.8 115.6 %finish.1 = bf16[512,2048]{1,0:T(8,128)(2,1)} custom-call(f32[8,128]{1,0:T(8,128)} %get-tuple-element.13.flag, bf16[512,2048]{1,0:T(8,128)(2,1)} %get-tuple-element.14.cand, bf16[512,2048]{1,0:T(8,128)(2,1)} %q_hbm.3, bf16[512,512]{1,0:T(8,128)(2,1)} %k_hbm.3, bf16[512,512]{1,0:T(8,128)(2,1)} %v_hbm.3, bf16[4,4,512,128]{3,2,1,0:T(8,128)(2,1)} %get-tuple-element.15.k_all, ...), custom_call_target="tpu_custom_call" | custom-call | tf_op jit(solution)/shard_map/finish/pallas_call | solution.py:739

commit v3 on v2

--- a/solution.py
+++ b/solution.py
@@ -23,7 +23,7 @@
 G = 4
 STATE_ROWS = H + 16
 ORDERS = (
-    ((1, 0), (3, 2), (3, 3), (1, 1), (3, 0), (3, 1), (2, 0), (1, 2), (2, 1), (2, 2), (1, 3), (2, 3)),
+    ((1, 0), (3, 2), (3, 3), (1, 1), (3, 0), (2, 0), (2, 2), (2, 1), (1, 2), (3, 1), (1, 3), (2, 3)),
     ((1, 0), (1, 1), (3, 2), (1, 2), (3, 3), (1, 3), (3, 0), (3, 1), (2, 0), (2, 1), (2, 2), (2, 3)),
     ((1, 0), (1, 1), (3, 0), (1, 2), (3, 1), (3, 2), (1, 3), (3, 3), (2, 0), (2, 1), (2, 2), (2, 3)),
     ((1, 0), (3, 2), (1, 1), (3, 3), (1, 2), (3, 0), (1, 3), (3, 1), (2, 0), (2, 1), (2, 2), (2, 3)),
@@ -159,28 +159,34 @@
         for kind in (0, 1):
             block_copy((kb, vb)[kind].at[head], back, head, kind, to_four).wait_recv()
 
+    def save_one(back, head, kind):
+        pltpu.make_async_copy(
+            (rk, rv)[kind].at[back - 1, head], (k_all, v_all)[kind].at[back - 1, head],
+            save_sem.at[back - 1, head, kind],
+        ).start()
+
     def save(back, head):
         for kind in (0, 1):
-            pltpu.make_async_copy(
-                (rk, rv)[kind].at[back - 1, head], (k_all, v_all)[kind].at[back - 1, head],
-                save_sem.at[back - 1, head, kind],
-            ).start()
-
-    def relay_four(step):
+            save_one(back, head, kind)
+
+    def relay_four(step, kind, up=True, down=True):
         head = early_head(step)
-        receive(4, head)
-        for kind in (0, 1):
-            held = (rk, rv)[kind].at[3, head]
+        held = (rk, rv)[kind].at[3, head]
+        if down:
+            block_copy(held, 4, head, kind, to_four).wait_recv()
+        if up:
 
             @pl.when(z == 3)
             def _():
                 block_copy(held, 1, head, kind, to_one).start()
 
+        if down:
+
             @pl.when(z > 0)
             def _():
                 block_copy(held, 3, head, kind, to_three).start()
 
-        save(4, head)
+            save_one(4, head, kind)
 
     def stop_copy(source, head, kind, target):
         slot = lax.rem(head, 2)
@@ -263,6 +269,7 @@
     last_id = id_row[:, T - 1 : T]
     own_tail = id_column == last_id
 
+    relay_four(0, 0)
     for back in (1, 2, 3, 4):
         id_copy(back).wait_recv()
     prev_id = jnp.where(me > 0, rid[0].astype(F32)[:, T - 1 : T], -1.0)
@@ -414,8 +421,15 @@
                 grown = jnp.exp2(scores * SCALE + later[here, since]).astype(BF16)
                 gather(here, at, nn(grown, wide[since]))
 
-    relay_four(0)
+    relay_four(0, 1)
     own_send(1, 1)
+
+    def first_up(head, at_end):
+        @pl.when((z == 3) == at_end)
+        def _():
+            receive(1, head)
+            relay_up(head)
+            save(1, head)
 
     def own_step(head, carry):
         own_unit(head)
@@ -428,18 +442,19 @@
         def _():
             after_line()
             own_send(2, 1)
+            first_up(0, True)
 
         @pl.when(head == 2)
         def _():
-            relay_four(1)
+            relay_four(1, 0)
+            relay_four(1, 1)
             own_send(3, 0)
 
         @pl.when(head == 3)
         def _():
             own_send(3, 1)
-            receive(1, 0)
-            relay_up(0)
-            save(1, 0)
+            first_up(0, False)
+            first_up(1, True)
 
         return carry
 
@@ -489,27 +504,37 @@
     def far_step(step, carry):
         back, head = listed(step)
 
-        @pl.when(step == 0)
+        @pl.when(step == 1)
         def _():
             after_x()
 
+        @pl.when(step == 3)
+        def _():
+            after_y()
+
         @pl.when(step == 1)
         def _():
-            relay_four(2)
+            relay_four(2, 0, up=False)
+            relay_four(2, 1, up=False)
 
         @pl.when(step == 2)
         def _():
-            after_y()
+            relay_four(2, 0, down=False)
+            relay_four(2, 1, down=False)
             hand_on(0, 0)
 
         @pl.when(step == 3)
         def _():
-            relay_four(3)
+            relay_four(3, 0)
+            relay_four(3, 1)
 
         @pl.when(step == 6)
         def _():
             hand_on(1, 0)
             hand_on(0, 3)
+
+        @pl.when(step == 7)
+        def _():
             cross()
 
         @pl.when(step == 8)
@@ -520,12 +545,12 @@
             inverse_out[...] = lax.rsqrt(mean + 1e-06)
             flag[...] = jnp.zeros((8, H), F32)
 
-        @pl.when((back != 1) | (head != 0))
+        @pl.when((back != 1) | (head > jnp.where(z == 3, 1, 0)))
         def _():
             receive(back, head)
             save(back, head)
 
-        @pl.when((back == 1) & (head == 1))
+        @pl.when((back == 1) & (head == 1) & (z < 3))
         def _():
             relay_up(head)
 
@@ -544,6 +569,7 @@
     def last_step(step, carry):
         far_step(step, carry)
         head = step - 8
+        head = jnp.where((z == 0) & (head > 0) & (head < 3), 3 - head, head)
         for member in range(G):
             at = head_columns(head * G + member)
             mass = total[:, at]

time: 189 us -> 188 us (level)
  Pallas kernels: 187 us -> 185 us
    pallas_call x1, Pallas kernels: 71.8 us -> 69.3 us  [body(): pl.pallas_call(main_kernel, out_shape=(jax.ShapeDtypeStruct((T, wide), BF...]
where the time goes in v3:
time: 188 us; the launch traced here: 185 us
  Pallas kernels  185 us (98%)
    pallas_call x1, Pallas kernels, body(): pl.pallas_call(finish_kernel, out_shape=jax.ShapeDtypeStruct((T, wide), B...  116 us
    pallas_call x1, Pallas kernels, body(): pl.pallas_call(main_kernel, out_shape=(jax.ShapeDtypeStruct((T, wide), BF...  69.3 us

profile of v3, /device:TPU:1, one launch (start us, length us, event | category | flops | bytes accessed | tf_op | source)
XLA Modules:
  0.0 185.0 jit_solution(14277097676600230381)
XLA Ops:
  0.0 69.3 %attend.1 = (bf16[512,2048]{1,0:T(8,128)(2,1)}, f32[8,128]{1,0:T(8,128)}, bf16[4,4,512,128]{3,2,1,0:T(8,128)(2,1)}, bf16[4,4,512,128]{3,2,1,0:T(8,128)(2,1)}, f3...) custom-call(bf16[512,2048]{1,0:T(8,128)(2,1)} %q_hbm.3, ...), custom_call_target="tpu_custom_call" | custom-call | tf_op jit(solution)/shard_map/attend/pallas_call | solution.py:702
  69.3 115.5 %finish.1 = bf16[512,2048]{1,0:T(8,128)(2,1)} custom-call(f32[8,128]{1,0:T(8,128)} %get-tuple-element.13.flag, bf16[512,2048]{1,0:T(8,128)(2,1)} %get-tuple-element.14.cand, bf16[512,2048]{1,0:T(8,128)(2,1)} %q_hbm.3, bf16[512,512]{1,0:T(8,128)(2,1)} %k_hbm.3, bf16[512,512]{1,0:T(8,128)(2,1)} %v_hbm.3, bf16[4,4,512,128]{3,2,1,0:T(8,128)(2,1)} %get-tuple-element.15.k_all, ...), custom_call_target="tpu_custom_call" | custom-call | tf_op jit(solution)/shard_map/finish/pallas_call | solution.py:765

commit v4 on v3

--- a/solution.py
+++ b/solution.py
@@ -23,7 +23,7 @@
 G = 4
 STATE_ROWS = H + 16
 ORDERS = (
-    ((1, 0), (3, 2), (3, 3), (1, 1), (3, 0), (2, 0), (2, 2), (2, 1), (1, 2), (3, 1), (1, 3), (2, 3)),
+    ((1, 0), (3, 2), (3, 3), (1, 1), (3, 0), (2, 0), (3, 1), (2, 2), (1, 2), (2, 1), (1, 3), (2, 3)),
     ((1, 0), (1, 1), (3, 2), (1, 2), (3, 3), (1, 3), (3, 0), (3, 1), (2, 0), (2, 1), (2, 2), (2, 3)),
     ((1, 0), (1, 1), (3, 0), (1, 2), (3, 1), (3, 2), (1, 3), (3, 3), (2, 0), (2, 1), (2, 2), (2, 3)),
     ((1, 0), (3, 2), (1, 1), (3, 3), (1, 2), (3, 0), (1, 3), (3, 1), (2, 0), (2, 1), (2, 2), (2, 3)),

time: 188 us -> 186 us (0.989); the launches traced: 185 us -> 185 us
  no operation moved by 1% of the time
where the time goes in v4:
time: 186 us; the launch traced here: 185 us
  Pallas kernels  185 us (99%)
    pallas_call x1, Pallas kernels, body(): pl.pallas_call(finish_kernel, out_shape=jax.ShapeDtypeStruct((T, wide), B...  116 us
    pallas_call x1, Pallas kernels, body(): pl.pallas_call(main_kernel, out_shape=(jax.ShapeDtypeStruct((T, wide), BF...  69.4 us

profile of v4, /device:TPU:1, one launch (start us, length us, event | category | flops | bytes accessed | tf_op | source)
XLA Modules:
  0.0 185.2 jit_solution(12546110051400259332)
XLA Ops:
  0.0 69.4 %attend.1 = (bf16[512,2048]{1,0:T(8,128)(2,1)}, f32[8,128]{1,0:T(8,128)}, bf16[4,4,512,128]{3,2,1,0:T(8,128)(2,1)}, bf16[4,4,512,128]{3,2,1,0:T(8,128)(2,1)}, f3...) custom-call(bf16[512,2048]{1,0:T(8,128)(2,1)} %q_hbm.3, ...), custom_call_target="tpu_custom_call" | custom-call | tf_op jit(solution)/shard_map/attend/pallas_call | solution.py:702
  69.5 115.5 %finish.1 = bf16[512,2048]{1,0:T(8,128)(2,1)} custom-call(f32[8,128]{1,0:T(8,128)} %get-tuple-element.13.flag, bf16[512,2048]{1,0:T(8,128)(2,1)} %get-tuple-element.14.cand, bf16[512,2048]{1,0:T(8,128)(2,1)} %q_hbm.3, bf16[512,512]{1,0:T(8,128)(2,1)} %k_hbm.3, bf16[512,512]{1,0:T(8,128)(2,1)} %v_hbm.3, bf16[4,4,512,128]{3,2,1,0:T(8,128)(2,1)} %get-tuple-element.15.k_all, ...), custom_call_target="tpu_custom_call" | custom-call | tf_op jit(solution)/shard_map/finish/pallas_call | solution.py:765
